TPU v7x, 256 devices: a whole 4x4x8 slice. The times are simulated.
256 devices in a mesh: dp: 16 (over z_hi, x, core), tensor: 16 (over z_lo, y).
Axes of the slice: x: 4, y: 4, z: 8 (z_hi: 2, z_lo: 4; z = z_hi * 4 + z_lo), core: 2. Of those that a mesh axis runs over, the one named last changes fastest.
Arguments:
- train_hidden: bfloat16 [48, 256, 28672], P('dp', None, 'tensor'), may hold values from -6 to 6
- train_grad: bfloat16 [48, 256, 8192], P('dp', None, 'tensor'), may hold values from -6 to 6
- val_hidden: bfloat16 [16, 128, 28672], P('dp', None, 'tensor'), may hold values from -6 to 6
- val_grad: bfloat16 [16, 128, 8192], P('dp', None, 'tensor'), may hold values from -6 to 6
- train_lengths: int32 [48], P('dp'), may hold values from 1 to 256, as said below
- train_buckets: int32 [48], P('dp'), may hold values from 0 to 3, as said below
- val_lengths: int32 [16], replicated, may hold values from 1 to 128, as said below
- bucket_weight: float32 [4], replicated, may hold values from 0.5 to 2
Outputs:
- scores: float32 [48, 16], P('dp')
Inputs may be any that keep to these rules, and one draw needn't show every extreme that they name: `train_lengths`: bucket b holds lengths from b * 64 + 1 to (b + 1) * 64; some prompt of bucket 3 has exactly 256 tokens. `train_buckets`: both the first and the last bucket occur. `val_lengths`: some validation prompt has exactly 128 tokens.
All inputs are finite; a program needn't handle non-finite values.
Results may differ from a plain program's by a relative error of at most 0.0003.
Values may be sent and summed in bfloat16 or wider, within the bound.
A program may use at most 128 MiB of HBM per device.

v0:
```python
import math

import jax
import jax.numpy as jnp
from jax import lax
from jax.sharding import PartitionSpec as P

D = 8192
FF = 28672
V_DEV = 1


def local(
    train_hidden,
    train_grad,
    val_hidden,
    val_grad,
    train_lengths,
    train_buckets,
    val_lengths,
    bucket_weight,
):
    prompts = train_hidden.shape[0]
    slots = train_hidden.shape[1]
    val_slots = val_hidden.shape[1]
    val_total = val_lengths.shape[0]
    own_val = lax.dynamic_slice_in_dim(val_lengths, lax.axis_index("dp") * V_DEV, V_DEV, 0)
    train_mask = jnp.arange(slots)[None, :] < train_lengths[:, None]
    train_masked = jnp.where(train_mask[:, :, None], train_hidden, jnp.zeros((), jnp.bfloat16))
    val_mask = jnp.arange(val_slots)[None, :] < own_val[:, None]
    val_masked = jnp.where(val_mask[:, :, None], val_hidden, jnp.zeros((), jnp.bfloat16))
    all_hidden, all_grad = (
        lax.all_gather(val_masked, "dp", axis=0, tiled=True),
        lax.all_gather(val_grad, "dp", axis=0, tiled=True),
    )
    train_flat = train_masked.reshape(prompts * slots, train_hidden.shape[2])
    grad_flat = train_grad.reshape(prompts * slots, train_grad.shape[2])
    val_flat = all_hidden.reshape(val_total * val_slots, all_hidden.shape[2])
    val_grad_flat = all_grad.reshape(val_total * val_slots, all_grad.shape[2])
    contract = (((1,), (1,)), ((), ()))
    hidden_gram = lax.dot_general(
        train_flat, val_flat, contract, preferred_element_type=jnp.float32
    )
    grad_gram = lax.dot_general(
        grad_flat, val_grad_flat, contract, preferred_element_type=jnp.float32
    )
    width = lax.axis_size("tensor")
    row_ids = jnp.arange(prompts * slots)
    col_ids = jnp.arange(val_total * val_slots)
    hidden_part, grad_part = (
        lax.psum_scatter(hidden_gram, "tensor", scatter_dimension=0, tiled=True),
        lax.psum_scatter(grad_gram, "tensor", scatter_dimension=0, tiled=True),
    )
    share = prompts * slots // width
    row_ids = lax.axis_index("tensor") * share + jnp.arange(share)
    product = hidden_part * grad_part
    row_owner = (row_ids[:, None] // slots == jnp.arange(prompts)[None, :]).astype(jnp.float32)
    col_owner = (col_ids[:, None] // val_slots == jnp.arange(val_total)[None, :]).astype(
        jnp.float32
    )
    by_prompt = jnp.dot(
        row_owner.T, product, precision=lax.Precision.HIGHEST, preferred_element_type=jnp.float32
    )
    partial_sum = jnp.dot(
        by_prompt, col_owner, precision=lax.Precision.HIGHEST, preferred_element_type=jnp.float32
    )
    pair_sum = lax.psum(partial_sum, "tensor")
    chosen = (train_buckets[:, None] == jnp.arange(bucket_weight.shape[0])[None, :]).astype(
        jnp.float32
    )
    weight = jnp.sum(chosen * bucket_weight[None, :], axis=1)
    counts = train_lengths.astype(jnp.float32)[:, None] * val_lengths.astype(jnp.float32)[None, :]
    return pair_sum * weight[:, None] / (math.sqrt(FF * D) * jnp.sqrt(counts))


def solution(mesh):
    placed = (
        P("dp", None, "tensor"),
        P("dp", None, "tensor"),
        P("dp", None, "tensor"),
        P("dp", None, "tensor"),
        P("dp"),
        P("dp"),
        P(),
        P(),
    )
    return jax.shard_map(
        local, mesh=mesh, in_specs=placed, out_specs=P("dp", None), check_vma=False
    )
```

profile of v0, /device:TPU:6, one launch (start us, length us, event | category | flops | bytes accessed | tf_op | source)
XLA Modules:
  0.0 421.0 jit_solution(15507376425999143011)
XLA Ops:
  6.5 0.0 copy-start
  6.5 0.0 all-gather.5.cloned.1.call-start
  6.5 0.7 all-gather.5.cloned.1.call-update
  7.3 0.0 all-gather.3.cloned.1.call-start
  7.3 1.2 dynamic_slice.3
  8.6 0.6 iota_compare_fusion.6
  9.2 1.9 broadcast_select_fusion.1
  11.1 0.0 all-gather.3.cloned.1.call-update
  11.1 0.0 reduce-scatter.5.cloned.1.call-start
  11.2 64.5 %all-gather.5.cloned.1.call-done = bf16[16,128,512]{2,1,0:T(8,128)(2,1)} async-done(((bf16[1,128,512]{2,1,0:T(8,128)(2,1)}), bf16[16,128,512]{2,1,0:T(8,128)(2,1)}) %all-gather.5.cloned.1.call-update) | async-done | bytes 2097168 | tf_op jit(solution)/shard_map/all_gather | solution.py:34
  75.6 0.0 copy-done
  75.6 6.1 %fusion.9 = f32[768,2048]{1,0:T(8,128)} fusion(bf16[768,512]{1,0:T(8,128)(2,1)S(1)} %bitcast.10, bf16[2048,512]{1,0:T(8,128)(2,1)} %bitcast.12), kind=kOutput, calls=%fused_computation.26 | convolution fusion | flops 1610612736 | bytes 9175040 | tf_op jit(solution)/shard_map/dot_general | solution.py:44
  81.7 0.0 copy-start.3
  81.7 0.0 copy-start.1
  81.7 0.0 reduce-scatter.5.cloned.1.call-update
  81.8 0.0 reduce-scatter.3.cloned.1.call-start
  81.8 0.6 copy-done.3
  82.4 0.1 iota_compare_fusion.4
  82.5 1.1 copy-done.1
  83.5 1.8 broadcast_select_fusion
  85.4 88.2 %all-gather.3.cloned.1.call-done = bf16[16,128,1792]{2,1,0:T(8,128)(2,1)} async-done(((bf16[1,128,1792]{2,1,0:T(8,128)(2,1)}), bf16[16,128,1792]{2,1,0:T(8,128)(2,1)}) %all-gather.3.cloned.1.call-update) | async-done | bytes 7340048 | tf_op jit(solution)/shard_map/all_gather | solution.py:33
  173.6 10.7 %fusion.8 = f32[768,2048]{1,0:T(8,128)} fusion(bf16[768,1792]{1,0:T(8,128)(2,1)} %bitcast.11, bf16[2048,1792]{1,0:T(8,128)(2,1)} %bitcast.13), kind=kOutput, calls=%fused_computation.25 | convolution fusion | flops 5637144576 | bytes 16384000 | tf_op jit(solution)/shard_map/dot_general | solution.py:41
  184.2 0.0 copy-start.2
  184.2 0.0 copy-start.4
  184.2 0.0 copy-start.5
  184.3 0.0 reduce-scatter.3.cloned.1.call-update
  184.3 0.6 copy-done.2
  184.9 0.0 copy-done.4
  184.9 0.0 copy-done.5
  184.9 0.2 select_reduce_fusion
  185.1 87.1 %reduce-scatter.5.cloned.1.call-done = f32[48,2048]{1,0:T(8,128)} async-done(((f32[768,2048]{1,0:T(8,128)}), f32[48,2048]{1,0:T(8,128)}) %reduce-scatter.5.cloned.1.call-update) | async-done | bytes 393232 | tf_op jit(solution)/shard_map/reduce_scatter | solution.py:52
  272.2 98.6 %reduce-scatter.3.cloned.1.call-done = f32[48,2048]{1,0:T(8,128)} async-done(((f32[768,2048]{1,0:T(8,128)}), f32[48,2048]{1,0:T(8,128)}) %reduce-scatter.3.cloned.1.call-update) | async-done | bytes 393232 | tf_op jit(solution)/shard_map/reduce_scatter | solution.py:51
  370.8 1.4 fusion.2
  372.3 0.6 fusion
  372.8 41.0 %psum.7 = f32[3,16]{1,0:T(4,128)S(1)} all-reduce(f32[3,16]{1,0:T(4,128)S(1)} %fusion), channel_id=1, replica_groups=mesh['dp'=16,'tensor'=16] {'tensor'}, use_global_device_ids=true, to_apply=%region_2.3 | all-reduce | flops 48 | bytes 384 | tf_op jit(solution)/shard_map/psum | solution.py:67
  413.9 0.7 multiply_divide_fusion
  (4 shorter events, 0.0 us)
Async XLA Ops:
  6.5 69.1 %copy-start = (bf16[3,256,512]{2,1,0:T(8,128)(2,1)S(1)}, bf16[3,256,512]{2,1,0:T(8,128)(2,1)}, u32[]{:S(2)}) copy-start(bf16[3,256,512]{2,1,0:T(8,128)(2,1)} %param.9) | copy-start | bytes 2359300
  6.5 69.1 %all-gather.5.cloned.1.call-start = ((), (), s32[]{:S(2)}) async-start(), calls=%async_computation.4 | async-start | bytes 2228224 | tf_op jit(solution)/shard_map/all_gather | solution.py:34
  7.3 166.3 %all-gather.3.cloned.1.call-start = ((), (), s32[]{:S(2)}) async-start(), calls=%async_computation.2 | async-start | bytes 7798784 | tf_op jit(solution)/shard_map/all_gather | solution.py:33
  11.1 261.1 %reduce-scatter.5.cloned.1.call-start = ((), (), s32[]{:S(2)}) async-start(), calls=%async_computation.5 | async-start | bytes 6684672 | tf_op jit(solution)/shard_map/reduce_scatter | solution.py:52
  81.7 0.7 copy-start.3
  81.7 1.8 copy-start.1
  81.8 289.1 %reduce-scatter.3.cloned.1.call-start = ((), (), s32[]{:S(2)}) async-start(), calls=%async_computation.3 | async-start | bytes 6684672 | tf_op jit(solution)/shard_map/reduce_scatter | solution.py:51
  184.2 0.7 copy-start.2
  184.2 0.7 copy-start.4
  184.2 0.7 copy-start.5
Sparse Core Ops, SparseCore 0:
  10.1 65.5 all-gather.4
  78.4 95.1 all-gather.2
  176.1 96.0 reduce-scatter.4
  274.6 96.1 reduce-scatter.2
where the time goes:
time: 421 us
  waiting for transfers between devices  339 us (81%)
  blocking collectives  41 us (10%)
  matrix products  18.8 us (4%)
  between operations  13.2 us (3%)
  other arithmetic  5.29 us (1%)
    reduce_scatter x1, waiting for transfers between devices, local(): lax.psum_scatter(hidden_gram, 'tensor', scatter_dimension=0, tiled=True)  98.6 us
    all_gather x1, waiting for transfers between devices, local(): lax.all_gather(val_masked, 'dp', axis=0, tiled=True)  88.2 us
    reduce_scatter x1, waiting for transfers between devices, local(): lax.psum_scatter(grad_gram, 'tensor', scatter_dimension=0, tiled=True)  87.1 us
    all_gather x1, waiting for transfers between devices, local(): lax.all_gather(val_grad, 'dp', axis=0, tiled=True)  64.5 us
    psum x1, blocking collectives, local(): pair_sum = lax.psum(partial_sum, 'tensor')  41 us
    dot_general x1, matrix products, local(): lax.dot_general(train_flat, val_flat, contract, preferred_element_type=jn...  10.7 us
  transfers between devices with their start and end apart: 4, of which 4 were waited for; matrix products, arithmetic and copies ran while one was open for 5% of the time, Pallas kernels for 0%

commit v1 on v0

v1 whole, which is shorter than its diff:
```python
import functools
import math

import jax
import jax.numpy as jnp
from jax import lax
from jax.experimental import pallas as pl
from jax.experimental.pallas import tpu as pltpu
from jax.sharding import PartitionSpec as P

MESH = pl.DeviceIdType.MESH
D = 8192
FF = 28672
TOP = 32000.0
STEPS = 8.0
ROWS = 1536
HALF = 768
PIECE = 96
CODE = 16
SLOT = PIECE + CODE
RS_ROWS = (768, 384, 192, 96)
ORDER = (0, 1, 3, 2, 4, 5, 7, 6)


def quantize(x):
    top = jnp.maximum(jnp.max(jnp.abs(x), axis=0, keepdims=True), 1e-30)
    code = jnp.ceil(jnp.log2(top) * STEPS)
    q = jnp.round(x * (jnp.exp2(code * (-1.0 / STEPS)) * TOP)).astype(jnp.int32).astype(jnp.int16)
    return q, jnp.broadcast_to(code, (CODE, x.shape[1])).astype(jnp.int32).astype(jnp.int16)


def step_of(code):
    code = code.astype(jnp.int32).astype(jnp.float32)
    return jnp.exp2(code[:1] * (1.0 / STEPS)) * (1.0 / TOP)


def widen(q):
    return q.astype(jnp.int32).astype(jnp.float32)


def kernel(
    tl,
    tb,
    vl,
    bw,
    th,
    tg,
    vh,
    vg,
    out,
    th_b,
    tg_b,
    vh_b,
    vg_b,
    gram,
    hid,
    sb1,
    sb2,
    sb3,
    sb4,
    rb1,
    rb2,
    rb3,
    rb4,
    g_all,
    info,
    total,
    fin1,
    fin2,
    ssem,
    rsem,
    lsem,
):
    dp, tn = lax.axis_index("dp"), lax.axis_index("tensor")
    zh, x, c = dp // 8, (dp // 2) % 4, dp % 2
    zl, y = tn // 4, tn % 4

    def dev(zh=zh, x=x, c=c, zl=zl, y=y):
        return (zh * 8 + x * 2 + c, zl * 4 + y)

    sib = dev(c=1 - c)
    zhp = dev(zh=1 - zh)
    xp, xm, x2 = dev(x=(x + 1) % 4), dev(x=(x + 3) % 4), dev(x=(x + 2) % 4)
    y1, y3 = dev(y=y + 1 - 2 * (y % 2)), dev(y=3 - y)
    z1, z2 = dev(zl=zl + 1 - 2 * (zl % 2)), dev(zl=(zl + 2) % 4)
    fin_y = [
        dev(c=(c + dc) % 2, y=(y + dy) % 4) for dc in range(2) for dy in range(4) if dc + dy > 0
    ]
    fin_z = [dev(zl=(zl + dz) % 4) for dz in range(1, 4)]
    g0, g1 = (y % 2 + y // 2) % 2, y // 2
    z0, zb = zl % 2, zl // 2

    pending = []
    count = [0]

    def send(src, dst, to):
        i = count[0]
        count[0] += 1
        copy = pltpu.make_async_remote_copy(
            src_ref=src,
            dst_ref=dst,
            send_sem=ssem.at[i],
            recv_sem=rsem.at[i],
            device_id=to,
            device_id_type=MESH,
        )
        copy.start()
        pending.append(copy)
        return copy

    own = [
        pltpu.make_async_copy(vg, vg_b.at[pl.ds(0, 128)], lsem.at[0]),
        pltpu.make_async_copy(tg, tg_b.at[pl.ds(0, HALF)], lsem.at[1]),
        pltpu.make_async_copy(vh, vh_b.at[pl.ds(0, 128)], lsem.at[2]),
        pltpu.make_async_copy(th, th_b.at[pl.ds(0, HALF)], lsem.at[3]),
    ]
    for copy in own:
        copy.start()
    row8 = lax.broadcasted_iota(jnp.int32, (8, 128), 0)
    lane8 = lax.broadcasted_iota(jnp.int32, (8, 128), 1)
    info[0] = jnp.where(row8 == 0, tl[0], jnp.where(row8 == 1, tl[1], tl[2])).astype(jnp.float32)

    barrier = pltpu.get_barrier_semaphore()
    peers = [zhp, xp, xm, x2, z1, z2, fin_z[2]] + fin_y
    peers = [zhp, xp, xm, x2] + fin_z + fin_y
    for peer in peers:
        pl.semaphore_signal(barrier, inc=1, device_id=peer, device_id_type=MESH)
    pl.semaphore_wait(barrier, len(peers))

    def vslot(ref, s, half=None):
        return ref.at[pl.ds(128 * s, 128)] if half is None else ref.at[pl.ds(128 * s + 64 * half, 64)]

    arrived = {}
    arrived["g4"] = send(vg, vslot(vg_b, 4), zhp)
    arrived["g1"] = send(vg, vslot(vg_b, 1), xp)
    arrived["g3"] = send(vg, vslot(vg_b, 3), xm)
    arrived["g2"] = send(vg, vslot(vg_b, 2), x2)
    arrived["tg"] = send(tg, tg_b.at[pl.ds(HALF, HALF)], sib)
    arrived["info"] = send(info.at[0], info.at[1], sib)

    def vh_half(h):
        return vh.at[pl.ds(64 * h, 64)]

    ops = []

    def at(time, fn):
        ops.append((time, len(ops), fn))

    def start_hidden():
        arrived["h4", 0] = send(vh_half(0), vslot(vh_b, 4, 0), zhp)
        arrived["h1", 0] = send(vh_half(0), vslot(vh_b, 1, 0), xp)
        arrived["h3", 1] = send(vh_half(1), vslot(vh_b, 3, 1), xm)
        arrived["th"] = send(th, th_b.at[pl.ds(HALF, HALF)], sib)
        arrived["h1", 1] = send(vh_half(1), vslot(vh_b, 1, 1), xp)
        arrived["h3", 0] = send(vh_half(0), vslot(vh_b, 3, 0), xm)
        arrived["h4", 1] = send(vh_half(1), vslot(vh_b, 4, 1), zhp)

    at(3.0, start_hidden)

    def forward_own():
        arrived["h1", 0].wait_recv()
        arrived["h2", 0] = send(vslot(vh_b, 1, 0), vslot(vh_b, 2, 0), xp)
        arrived["h3", 1].wait_recv()
        arrived["h2", 1] = send(vslot(vh_b, 3, 1), vslot(vh_b, 2, 1), xm)

    at(16.0, forward_own)

    def forward_far(h):
        arrived["h4", h].wait_recv()
        arrived["h5", h] = send(vslot(vh_b, 4, h), vslot(vh_b, 5, h), xp)
        arrived["h7", h] = send(vslot(vh_b, 4, h), vslot(vh_b, 7, h), xm)

    at(21.0, lambda: forward_far(0))
    at(29.0, lambda: forward_far(1))

    def forward_last():
        arrived["h5", 0].wait_recv()
        arrived["h6", 0] = send(vslot(vh_b, 5, 0), vslot(vh_b, 6, 0), xp)
        arrived["h7", 1].wait_recv()
        arrived["h6", 1] = send(vslot(vh_b, 7, 1), vslot(vh_b, 6, 1), xm)

    at(38.0, forward_last)

    def forward_grad():
        arrived["g4"].wait_recv()
        arrived["g5"] = send(vslot(vg_b, 4), vslot(vg_b, 5), xp)
        arrived["g7"] = send(vslot(vg_b, 4), vslot(vg_b, 7), xm)
        arrived["g6"] = send(vslot(vg_b, 4), vslot(vg_b, 6), x2)

    at(10.5, forward_grad)

    def mask_train():
        own[1].wait()
        arrived["info"].wait_recv()
        arrived["tg"].wait_recv()
        token = lax.broadcasted_iota(jnp.int32, (256, 128), 0).astype(jnp.float32)
        for i in range(6):
            keep = token < info[i // 3, i % 3 : i % 3 + 1, :]
            rows = pl.ds(256 * i, 256)
            for j in range(4):
                cols = pl.ds(128 * j, 128)
                tg_b[rows, cols] = jnp.where(
                    keep, tg_b[rows, cols].astype(jnp.float32), 0.0
                ).astype(jnp.bfloat16)

    at(5.0, mask_train)

    contract = (((1,), (1,)), ((), ()))
    sbs, rbs = (sb1, sb2, sb3, sb4), (rb1, rb2, rb3, rb4)

    def way(k):
        if k % 2 == 0:
            return ((g0, y1), (g1, y3), (z0, z1), (zb, z2))
        return ((g1, y3), (g0, y1), (z0, z1), (zb, z2))

    def send_part(k, step, x):
        n = RS_ROWS[step]
        q, code = quantize(x)
        sbs[step][k, pl.ds(0, n), :] = q
        sbs[step][k, pl.ds(n, CODE), :] = code
        arrived["r", k, step] = send(sbs[step].at[k], rbs[step].at[k], way(k)[step][1])

    base = {}

    def begin(k):
        s = ORDER[k]
        if s == 0:
            own[0].wait()
        elif s != 4:
            arrived["g%d" % s].wait_recv()
        rhs = vg_b[pl.ds(128 * s, 128), :]

        @pl.loop(0, ROWS // 256)
        def _(i):
            rows = pl.ds(pl.multiple_of(i * 256, 256), 256)
            gram[k, rows, :] = lax.dot_general(
                tg_b[rows, :], rhs, contract, preferred_element_type=jnp.float32
            )

        bit = way(k)[0][0]
        base[k] = bit * 768
        send_part(k, 0, gram[k, pl.ds(pl.multiple_of((1 - bit) * 768, 768), 768), :])

    def middle(k, step):
        arrived["r", k, step - 1].wait_recv()
        n = RS_ROWS[step]
        bit = way(k)[step][0]
        got = rbs[step - 1]
        scale = step_of(got[k, pl.ds(2 * n, CODE), :])

        def summed(part):
            there = pl.ds(pl.multiple_of(base[k] + part * n, 96), n)
            here = pl.ds(pl.multiple_of(part * n, 96), n)
            return there, gram[k, there, :] + widen(got[k, here, :]) * scale

        send_part(k, step, summed(1 - bit)[1])
        there, kept = summed(bit)
        gram[k, there, :] = kept
        base[k] = base[k] + bit * n

    place = {}

    def ready(k):
        arrived["r", k, 3].wait_recv()
        scale = step_of(rb4[k, pl.ds(PIECE, CODE), :])
        there = pl.ds(pl.multiple_of(base[k], 96), PIECE)
        q, code = quantize(gram[k, there, :] + widen(rb4[k, pl.ds(0, PIECE), :]) * scale)
        b = [bit for bit, _ in way(k)]
        spots = [0]
        for i, bit in enumerate(b):
            spots.append(spots[-1] + bit * (8 >> i))
        place[k] = spots
        spot = pl.multiple_of(spots[4] * SLOT, CODE)
        g_all[k, pl.ds(spot, PIECE), :] = q
        g_all[k, pl.ds(pl.multiple_of(spot + PIECE, CODE), CODE), :] = code
        give(k, 3)

    def give(k, step):
        block = g_all.at[
            k, pl.ds(pl.multiple_of(place[k][step + 1] * SLOT, CODE), (8 >> step) * SLOT)
        ]
        arrived["a", k, step] = send(block, block, way(k)[step][1])

    def pass_on(k, step):
        arrived["a", k, step + 1].wait_recv()
        give(k, step)

    def times(k):
        pair = k // 2
        t0 = (6.0, 8.0, 9.0, 13.0, 20.0, 20.5, 26.0, 26.5)[k]
        return [t0, t0 + 7, t0 + 12, t0 + 16, t0 + 20, t0 + 23, t0 + 27, t0 + 32]

    for k in range(8):
        t = times(k)
        at(t[0], functools.partial(begin, k))
        for step in (1, 2, 3):
            at(t[step], functools.partial(middle, k, step))
        at(t[4], functools.partial(ready, k))
        for i, step in enumerate((2, 1, 0)):
            at(t[5 + i], functools.partial(pass_on, k, step))

    def hidden(k):
        s = ORDER[k]
        if k == 0:
            own[2].wait()
            own[3].wait()
            arrived["th"].wait_recv()
        for h in range(2):
            key = ("h%d" % s, h)
            if s != 0 and key not in waited:
                arrived[key].wait_recv()
        rhs = vh_b[pl.ds(128 * s, 128), :]

        @pl.loop(0, ROWS // 256)
        def _(i):
            rows = pl.ds(pl.multiple_of(i * 256, 256), 256)
            hid[k, rows, :] = lax.dot_general(
                th_b[rows, :], rhs, contract, preferred_element_type=jnp.float32
            )

    waited = {("h1", 0), ("h3", 1), ("h4", 0), ("h4", 1), ("h5", 0), ("h7", 1)}
    for k, t in enumerate((14.5, 22.0, 22.2, 27.0, 32.0, 44.0, 44.2, 46.0)):
        at(t, functools.partial(hidden, k))

    total[...] = jnp.zeros_like(total)

    def product(k):
        arrived["a", k, 0].wait_recv()
        s = ORDER[k]
        sums = [None] * 6
        for p in range(16):
            scale = step_of(g_all[k, pl.ds(p * SLOT + PIECE, CODE), :])
            both = hid[k, pl.ds(p * PIECE, PIECE), :] * widen(g_all[k, pl.ds(p * SLOT, PIECE), :])
            parts = {}
            for u in range(6):
                i = (p * 6 + u) // 16
                part = both[16 * u : 16 * u + 8] + both[16 * u + 8 : 16 * u + 16]
                parts[i] = part if i not in parts else parts[i] + part
            for i, part in parts.items():
                part = part * scale
                sums[i] = part if sums[i] is None else sums[i] + part
        tile = jnp.zeros((8, 128), jnp.float32)
        for i in range(6):
            tile = jnp.where(row8 == i, jnp.sum(sums[i], axis=0, keepdims=True), tile)
        far, r = s // 4, s % 4
        prompt = ((zh + far) % 2) * 8 + ((x + 4 - r) % 4) * 2 + c
        tile = jnp.where(lane8 < vl[prompt], tile, 0.0)
        total[...] += jnp.where(lane8 == prompt, jnp.sum(tile, axis=1, keepdims=True), 0.0)

    for k in range(8):
        at(max(times(k)[7] + 7, 46.5), functools.partial(product, k))

    for _, _, fn in sorted(ops, key=lambda op: op[:2]):
        fn()

    mine = total[...]
    turned = jnp.where(row8 < 3, pltpu.roll(mine, 5, 0), pltpu.roll(mine, 3, 0))
    fin1[0] = jnp.where(c == 0, mine, turned)
    last = [send(fin1.at[0], fin1.at[1 + i], peer) for i, peer in enumerate(fin_y)]
    for copy in last:
        copy.wait_recv()
    fin2[0] = jnp.sum(fin1[...], axis=0)
    last = [send(fin2.at[0], fin2.at[1 + i], peer) for i, peer in enumerate(fin_z)]
    for copy in last:
        copy.wait_recv()
    pair = jnp.sum(fin2[...], axis=0)
    pair = jnp.where(c == 0, pair, pltpu.roll(pair, 5, 0))
    weight = jnp.where(row8 == 0, bw[tb[0]], jnp.where(row8 == 1, bw[tb[1]], bw[tb[2]]))
    val_counts = jnp.ones((8, 128), jnp.float32)
    for j in range(16):
        val_counts = jnp.where(lane8 == j, vl[j].astype(jnp.float32), val_counts)
    scores = pair * weight / (math.sqrt(FF * D) * jnp.sqrt(info[0] * val_counts))
    out[...] = scores[:3, :16]
    for copy in pending:
        copy.wait_send()


def local(
    train_hidden,
    train_grad,
    val_hidden,
    val_grad,
    train_lengths,
    train_buckets,
    val_lengths,
    bucket_weight,
):
    smem = pl.BlockSpec(memory_space=pltpu.SMEM)
    hbm = pl.BlockSpec(memory_space=pl.ANY)
    n = 8
    i16, f32, bf16 = jnp.int16, jnp.float32, jnp.bfloat16
    copies = 8 * n + 7 + 14 + 3 + 10
    buffers = [pltpu.VMEM((n, r + CODE, 128), i16) for r in RS_ROWS]
    return pl.pallas_call(
        kernel,
        out_shape=jax.ShapeDtypeStruct((3, 16), f32),
        in_specs=[smem] * 4 + [hbm] * 4,
        out_specs=pl.BlockSpec(memory_space=pltpu.VMEM),
        scratch_shapes=[
            pltpu.VMEM((ROWS, 1792), bf16),
            pltpu.VMEM((ROWS, 512), bf16),
            pltpu.VMEM((1024, 1792), bf16),
            pltpu.VMEM((1024, 512), bf16),
            pltpu.VMEM((n, ROWS, 128), f32),
            pltpu.VMEM((n, ROWS, 128), f32),
            *buffers,
            *buffers,
            pltpu.VMEM((n, 16 * SLOT, 128), i16),
            pltpu.VMEM((2, 8, 128), f32),
            pltpu.VMEM((8, 128), f32),
            pltpu.VMEM((8, 8, 128), f32),
            pltpu.VMEM((4, 8, 128), f32),
            pltpu.SemaphoreType.DMA((copies,)),
            pltpu.SemaphoreType.DMA((copies,)),
            pltpu.SemaphoreType.DMA((4,)),
        ],
        compiler_params=pltpu.CompilerParams(
            collective_id=0, has_side_effects=True, vmem_limit_bytes=56 * 2**20
        ),
        name="ghost",
    )(
        train_lengths,
        train_buckets,
        val_lengths,
        bucket_weight,
        train_hidden.reshape(HALF, 1792),
        train_grad.reshape(HALF, 512),
        val_hidden.reshape(128, 1792),
        val_grad.reshape(128, 512),
    )


def solution(mesh):
    placed = (
        P("dp", None, "tensor"),
        P("dp", None, "tensor"),
        P("dp", None, "tensor"),
        P("dp", None, "tensor"),
        P("dp"),
        P("dp"),
        P(),
        P(),
    )
    return jax.shard_map(
        local, mesh=mesh, in_specs=placed, out_specs=P("dp", None), check_vma=False
    )
```

time: 421 us -> 110 us (0.26)
  waiting for transfers between devices: 339 us -> 0 us
  Pallas kernels: 0 us -> 109 us
  blocking collectives: 41 us -> 0 us
  matrix products: 18.8 us -> 0 us
  between operations: 13.2 us -> 0.01 us
  other arithmetic: 5.29 us -> 0 us
    reduce_scatter x2 -> x0, waiting for transfers between devices: 186 us -> none  [the longest x1 98.6 us: local(): lax.psum_scatter(hidden_gram, 'tensor', scatter_dimension=0, tiled=True)]
    all_gather x2 -> x0, waiting for transfers between devices: 153 us -> none  [the longest x1 88.2 us: local(): lax.all_gather(val_masked, 'dp', axis=0, tiled=True)]
    pallas_call x0 -> x1, Pallas kernels: none -> 109 us  [local(): pl.pallas_call(kernel, out_shape=jax.ShapeDtypeStruct((3, 16), f32), in_s...]
    psum x1 -> x0, blocking collectives: 41 us -> none  [local(): pair_sum = lax.psum(partial_sum, 'tensor')]
    dot_general x4 -> x0, matrix products: 18.8 us -> none  [the longest x1 10.7 us: local(): lax.dot_general(train_flat, val_flat, contract, preferred_element_type=jn...]
  transfers between devices with their start and end apart: 4 -> 0, of which waited for: 4 -> 0; matrix products, arithmetic and copies ran while one was open for 5% -> 0% of each run, Pallas kernels for 0% -> 0%
where the time goes in v1:
time: 110 us
  Pallas kernels  109 us (99%)
  local copies, waits for them, and re-layouts  1.26 us (1%)
    pallas_call x1, Pallas kernels, local(): pl.pallas_call(kernel, out_shape=jax.ShapeDtypeStruct((3, 16), f32), in_s...  109 us

profile of v1, /device:TPU:6, one launch (start us, length us, event | category | flops | bytes accessed | tf_op | source)
XLA Modules:
  0.0 110.0 jit_solution(5200397901162961097)
XLA Ops:
  0.0 108.7 %ghost.1 = f32[3,16]{1,0:T(4,128)} custom-call(s32[3]{0:T(128)} %tl.1, s32[3]{0:T(128)} %tb.1, s32[16]{0:T(128)} %vl.1, f32[4]{0:T(128)} %bw.1, bf16[768,1792]{1,0:T(8,128)(2,1)} %bitcast.4, bf16[768,512]{1,0:T(8,128)(2,1)} %bitcast.5, bf16[128,1792]{1,0:T(8,128)(2,1)} %bitcast.6, bf16[128,512]{1,0:T(8,128)(2,1)} %bitcast.7), custom_call_target="tpu_custom_call" | custom-call | tf_op jit(solution)/shard_map/ghost/pallas_call | solution.py:394
  108.7 1.3 %copy.10 = f32[3,16]{1,0:T(4,128)} copy(f32[3,16]{1,0:T(4,128)} %ghost.1) | data formatting | bytes 384

commit v2 on v0

v2 whole, which is shorter than its diff:
```python
import functools
import math

import jax
import jax.numpy as jnp
from jax import lax
from jax.experimental import pallas as pl
from jax.experimental.pallas import tpu as pltpu
from jax.sharding import PartitionSpec as P

MESH = pl.DeviceIdType.MESH
D = 8192
FF = 28672
TOP = 32000.0
STEPS = 8.0
ROWS = 1536
HALF = 768
PIECE = 96
CODE = 16
SLOT = PIECE + CODE
QUARTER = 384
BLOCK = QUARTER + CODE
UP = 192
TILE_G = 512
TILE_H = 512


def quantize(x):
    top = jnp.maximum(jnp.max(jnp.abs(x), axis=0, keepdims=True), 1e-30)
    code = jnp.ceil(jnp.log2(top) * STEPS)
    q = jnp.round(x * (jnp.exp2(code * (-1.0 / STEPS)) * TOP)).astype(jnp.int32).astype(jnp.int16)
    return q, jnp.broadcast_to(code, (CODE, x.shape[1])).astype(jnp.int32).astype(jnp.int16)


def step_of(code, rows=1):
    code = code.astype(jnp.int32).astype(jnp.float32)
    return jnp.exp2(code[:rows] * (1.0 / STEPS)) * (1.0 / TOP)


def widen(q):
    return q.astype(jnp.int32).astype(jnp.float32)


def kernel(
    n_near,
    n_far,
    tl,
    tb,
    vl,
    bw,
    th,
    tg,
    vh,
    vg,
    out,
    th_b,
    tg_b,
    vh_b,
    vg_b,
    gram,
    hid,
    pick,
    right_g,
    right_h,
    sy,
    ry,
    sz,
    rz,
    az,
    g_all,
    info,
    total,
    fin1,
    fin2,
    ssem,
    rsem,
    lsem,
):
    chunks = n_near + n_far
    dp, tn = lax.axis_index("dp"), lax.axis_index("tensor")
    zh, x, c = dp // 8, (dp // 2) % 4, dp % 2
    zl, y = tn // 4, tn % 4

    def dev(zh=zh, x=x, c=c, zl=zl, y=y):
        return (zh * 8 + x * 2 + c, zl * 4 + y)

    sib = dev(c=1 - c)
    zhp = dev(zh=1 - zh)
    xp, xm, x2 = dev(x=(x + 1) % 4), dev(x=(x + 3) % 4), dev(x=(x + 2) % 4)
    ys = [dev(y=(y + i) % 4) for i in (1, 2, 3)]
    zs = [dev(zl=(zl + i) % 4) for i in (1, 2, 3)]
    fin_y = [
        dev(c=(c + dc) % 2, y=(y + dy) % 4) for dc in range(2) for dy in range(4) if dc + dy > 0
    ]

    pending = []
    count = [0]

    def send(src, dst, to):
        i = count[0]
        count[0] += 1
        copy = pltpu.make_async_remote_copy(
            src_ref=src,
            dst_ref=dst,
            send_sem=ssem.at[i],
            recv_sem=rsem.at[i],
            device_id=to,
            device_id_type=MESH,
        )
        copy.start()
        pending.append(copy)
        return copy

    own = [
        pltpu.make_async_copy(vg, vg_b.at[pl.ds(0, 128)], lsem.at[0]),
        pltpu.make_async_copy(tg, tg_b.at[pl.ds(0, HALF)], lsem.at[1]),
        pltpu.make_async_copy(vh, vh_b.at[pl.ds(0, 128)], lsem.at[2]),
        pltpu.make_async_copy(th, th_b.at[pl.ds(0, HALF)], lsem.at[3]),
    ]
    for copy in own:
        copy.start()
    row8 = lax.broadcasted_iota(jnp.int32, (8, 128), 0)
    lane8 = lax.broadcasted_iota(jnp.int32, (8, 128), 1)
    info[0] = jnp.where(row8 == 0, tl[0], jnp.where(row8 == 1, tl[1], tl[2])).astype(jnp.float32)

    barrier = pltpu.get_barrier_semaphore()
    peers = [zhp, xp, xm, x2] + zs + fin_y
    for peer in peers:
        pl.semaphore_signal(barrier, inc=1, device_id=peer, device_id_type=MESH)
    pl.semaphore_wait(barrier, len(peers))

    def place(ref, s, part=0, parts=1):
        return ref.at[pl.ds(128 * s + 128 // parts * part, 128 // parts)]

    def piece(ref, part, parts):
        return ref.at[pl.ds(128 // parts * part, 128 // parts)]

    arrived = {}
    for h in range(2):
        arrived["g", 4, h] = send(piece(vg, h, 2), place(vg_b, 4, h, 2), zhp)
    arrived["g", 1] = send(vg, place(vg_b, 1), xp)
    arrived["g", 2] = send(vg, place(vg_b, 2), xm)
    arrived["g", 3] = send(vg, place(vg_b, 3), x2)
    arrived["tg"] = send(tg, tg_b.at[pl.ds(HALF, HALF)], sib)
    arrived["info"] = send(info.at[0], info.at[1], sib)

    prompts, lens, begins = [], [], []
    near = 0
    so_far = 0
    for s in range(8):
        r = (0, 1, 3, 2)[s % 4]
        prompt = ((zh + s // 4) % 2) * 8 + ((x + 4 - r) % 4) * 2 + c
        prompts.append(prompt)
        lens.append(vl[prompt])
        begins.append(so_far)
        so_far = so_far + lens[s]
        if s == 3:
            near = so_far
    near_done = jnp.minimum(near, 128 * n_near)
    everything = so_far

    def chunk_range(k):
        if k < n_near:
            return 128 * k, 0, 4
        return everything - 128 * (chunks - k), near_done, 8

    def fill_pick(k):
        start, least, places = chunk_range(k)
        row = lax.broadcasted_iota(jnp.int32, (128, 128), 0)
        col = lax.broadcasted_iota(jnp.int32, (128, 128), 1)
        for s in range(places):
            rank = col + begins[s]
            hit = (rank - start == row) & (col < lens[s]) & (rank >= least)
            pick[k, :, pl.ds(128 * s, 128)] = jnp.where(hit, 1.0, 0.0).astype(jnp.bfloat16)

    def packed(k, ref, places):
        return lax.dot_general(
            pick[k, :, pl.ds(0, 128 * places)],
            ref[pl.ds(0, 128 * places), :],
            (((1,), (0,)), ((), ())),
            preferred_element_type=jnp.float32,
        )

    ops = []

    def at(time, fn):
        ops.append((time, len(ops), fn))

    def start_far():
        for q in range(4):
            arrived["h", 4, q] = send(piece(vh, q, 4), place(vh_b, 4, q, 4), zhp)

    def start_near(h):
        arrived["h", 1, h] = send(piece(vh, h, 2), place(vh_b, 1, h, 2), xp)
        arrived["h", 2, 1 - h] = send(piece(vh, 1 - h, 2), place(vh_b, 2, 1 - h, 2), xm)

    def start_train():
        arrived["th"] = send(th, th_b.at[pl.ds(HALF, HALF)], sib)

    waited = set()

    def have(key):
        if key not in waited:
            waited.add(key)
            arrived[key].wait_recv()

    def forward_near():
        have(("h", 1, 0))
        arrived["h", 3, 0] = send(place(vh_b, 1, 0, 2), place(vh_b, 3, 0, 2), xp)
        have(("h", 2, 1))
        arrived["h", 3, 1] = send(place(vh_b, 2, 1, 2), place(vh_b, 3, 1, 2), xm)

    def forward_far(q):
        have(("h", 4, q))
        arrived["h", 5, q] = send(place(vh_b, 4, q, 4), place(vh_b, 5, q, 4), xp)
        arrived["h", 6, q] = send(place(vh_b, 4, q, 4), place(vh_b, 6, q, 4), xm)

    def forward_last(q):
        s, to = (5, xp) if q % 2 == 0 else (6, xm)
        have(("h", s, q))
        arrived["h", 7, q] = send(place(vh_b, s, q, 4), place(vh_b, 7, q, 4), to)

    def forward_grad(h):
        have(("g", 4, h))
        for s, to in ((5, xp), (6, xm), (7, x2)):
            arrived["g", s, h] = send(place(vg_b, 4, h, 2), place(vg_b, s, h, 2), to)

    def mask_train():
        own[1].wait()
        have("info")
        have("tg")
        token = lax.broadcasted_iota(jnp.int32, (256, 128), 0).astype(jnp.float32)
        for i in range(6):
            keep = token < info[i // 3, i % 3 : i % 3 + 1, :]
            rows = pl.ds(256 * i, 256)
            for j in range(4):
                cols = pl.ds(128 * j, 128)
                tg_b[rows, cols] = jnp.where(
                    keep, tg_b[rows, cols].astype(jnp.float32), 0.0
                ).astype(jnp.bfloat16)

    def multiply(ks, left, ref, places, right, tile, to):
        for j, k in enumerate(ks):
            right[:, pl.ds(128 * j, 128)] = packed(k, ref, places).T.astype(jnp.bfloat16)

        @pl.loop(0, ROWS // tile)
        def _(i):
            rows = pl.ds(pl.multiple_of(i * tile, tile), tile)
            both = jnp.dot(
                left[rows, :],
                right[:, pl.ds(0, 128 * len(ks))],
                preferred_element_type=jnp.float32,
            )
            for j, k in enumerate(ks):
                to[k, rows, :] = both[:, 128 * j : 128 * j + 128]

    def put(ref, index, x):
        n = x.shape[0]
        q, code = quantize(x)
        ref[*index, pl.ds(0, n), :] = q
        ref[*index, pl.ds(n, CODE), :] = code

    def begin(ks):
        places = chunk_range(ks[0])[2]
        if 0 in ks:
            own[0].wait()
        for s in range(1, places):
            for key in (("g", s),) if s < 4 else (("g", s, 0), ("g", s, 1)):
                have(key)
        for k in ks:
            fill_pick(k)
        multiply(ks, tg_b, vg_b, places, right_g, TILE_G, gram)
        for k in ks:
            for i in range(3):
                theirs = pl.multiple_of(((y + 1 + i) % 4) * QUARTER, QUARTER)
                put(sy, (k, i), gram[k, pl.ds(theirs, QUARTER), :])
                arrived["y", k, i] = send(sy.at[k, i], ry.at[k, i], ys[i])

    def middle(k):
        for i in range(3):
            have(("y", k, i))
        scales = [step_of(ry[k, i, pl.ds(QUARTER, CODE), :]) for i in range(3)]

        def summed(part):
            here = pl.ds(pl.multiple_of(part * PIECE, PIECE), PIECE)
            there = pl.ds(pl.multiple_of(y * QUARTER + part * PIECE, PIECE), PIECE)
            value = gram[k, there, :]
            for i in range(3):
                value = value + widen(ry[k, i, here, :]) * scales[i]
            return there, value

        for i in range(3):
            put(sz, (k, i), summed((zl + 1 + i) % 4)[1])
            arrived["z", k, i] = send(sz.at[k, i], rz.at[k, i], zs[i])
        there, value = summed(zl)
        gram[k, there, :] = value

    def ready(k):
        for i in range(3):
            have(("z", k, i))
        there = pl.ds(pl.multiple_of(y * QUARTER + zl * PIECE, PIECE), PIECE)
        value = gram[k, there, :]
        for i in range(3):
            scale = step_of(rz[k, i, pl.ds(PIECE, CODE), :])
            value = value + widen(rz[k, i, pl.ds(0, PIECE), :]) * scale
        put(az, (k, 0), value)
        for i in range(3):
            arrived["az", k, i] = send(az.at[k, 0], az.at[k, 1 + i], zs[i])

    def block(k, i, first=0, rows=BLOCK):
        owner = (y + i) % 4
        return g_all.at[k, pl.ds(pl.multiple_of(owner * BLOCK + first, CODE), rows)]

    def spread(k):
        for i in range(3):
            have(("az", k, i))
        codes = jnp.zeros((CODE, 128), jnp.int32)
        row = lax.broadcasted_iota(jnp.int32, (CODE, 128), 0)
        for i in range(4):
            part = (zl + 4 - i) % 4
            spot = pl.multiple_of(y * BLOCK + part * PIECE, CODE)
            g_all[k, pl.ds(spot, PIECE), :] = az[k, i, pl.ds(0, PIECE), :]
            code = az[k, i, pl.ds(PIECE, CODE), :].astype(jnp.int32)
            codes = jnp.where(row == part, code, codes)
        g_all[k, pl.ds(pl.multiple_of(y * BLOCK + QUARTER, CODE), CODE), :] = codes.astype(jnp.int16)
        arrived["up", k] = send(block(k, 0), block(k, 0), ys[0])
        arrived["down", k] = send(block(k, 0), block(k, 0), ys[2])

    def relay(k):
        have(("up", k))
        rows = block(k, 3, 0, UP)
        arrived["up2", k] = send(rows, rows, ys[0])
        have(("down", k))
        rows = block(k, 1, UP, BLOCK - UP)
        arrived["down2", k] = send(rows, rows, ys[2])

    def hidden(ks):
        near_only, last = ks[-1] < n_near, ks[-1] == chunks - 1
        places = 4 if near_only else 8 if last else 7
        if 0 in ks:
            own[2].wait()
            own[3].wait()
            have("th")
        for s in range(1, places):
            for i in range(2 if s < 4 else 4):
                have(("h", s, i))
        multiply(ks, th_b, vh_b, places, right_h, TILE_H, hid)

    total[...] = jnp.zeros_like(total)

    def product(k):
        have(("up2", k))
        have(("down2", k))
        sums = [None] * 6
        for p in range(16):
            top = p // 4 * BLOCK
            if p % 4 == 0:
                steps = step_of(g_all[k, pl.ds(top + QUARTER, CODE), :], 8)
            scale = steps[p % 4 : p % 4 + 1]
            here = pl.ds(top + p % 4 * PIECE, PIECE)
            both = hid[k, pl.ds(p * PIECE, PIECE), :] * widen(g_all[k, here, :])
            parts = {}
            for u in range(6):
                i = (p * 6 + u) // 16
                part = both[16 * u : 16 * u + 8] + both[16 * u + 8 : 16 * u + 16]
                parts[i] = part if i not in parts else parts[i] + part
            for i, part in parts.items():
                part = part * scale
                sums[i] = part if sums[i] is None else sums[i] + part
        tile = jnp.zeros((8, 128), jnp.float32)
        for i in range(6):
            tile = jnp.where(row8 == i, jnp.sum(sums[i], axis=0, keepdims=True), tile)
        start, least, places = chunk_range(k)
        rank = lane8 + start
        for s in range(places):
            mine = (rank >= begins[s]) & (rank < begins[s] + lens[s]) & (rank >= least)
            total[s] += jnp.where(mine, tile, 0.0)

    do = dict(
        start_far=start_far,
        start_near=start_near,
        start_train=start_train,
        forward_near=forward_near,
        forward_far=forward_far,
        forward_last=forward_last,
        forward_grad=forward_grad,
        mask_train=mask_train,
        begin=begin,
        middle=middle,
        ready=ready,
        spread=spread,
        relay=relay,
        hidden=hidden,
        product=product,
    )
    plan(chunks, n_near, at, do)
    for _, _, fn in sorted(ops, key=lambda op: op[:2]):
        fn()

    mine = jnp.zeros((8, 128), jnp.float32)
    for s in range(8):
        mine = jnp.where(lane8 == prompts[s], jnp.sum(total[s], axis=1, keepdims=True), mine)
    turned = jnp.where(row8 < 3, pltpu.roll(mine, 5, 0), pltpu.roll(mine, 3, 0))
    fin1[0] = jnp.where(c == 0, mine, turned)
    last = [send(fin1.at[0], fin1.at[1 + i], peer) for i, peer in enumerate(fin_y)]
    for copy in last:
        copy.wait_recv()
    fin2[0] = jnp.sum(fin1[...], axis=0)
    last = [send(fin2.at[0], fin2.at[1 + i], peer) for i, peer in enumerate(zs)]
    for copy in last:
        copy.wait_recv()
    pair = jnp.sum(fin2[...], axis=0)
    pair = jnp.where(c == 0, pair, pltpu.roll(pair, 5, 0))
    weight = jnp.where(row8 == 0, bw[tb[0]], jnp.where(row8 == 1, bw[tb[1]], bw[tb[2]]))
    val_counts = jnp.ones((8, 128), jnp.float32)
    for j in range(16):
        val_counts = jnp.where(lane8 == j, vl[j].astype(jnp.float32), val_counts)
    scores = pair * weight / (math.sqrt(FF * D) * jnp.sqrt(info[0] * val_counts))
    out[...] = scores[:3, :16]
    for copy in pending:
        copy.wait_send()


def plan(chunks, n_near, at, do):
    def add(time, name, *args):
        at(time, functools.partial(do[name], *args))

    add(0.0, "start_far")
    add(0.1, "start_train")
    add(0.2, "start_near", 0)
    add(16.0, "mask_train")
    add(19.0, "forward_grad", 0)
    add(21.0, "forward_grad", 1)
    add(21.1, "start_near", 1)
    add(29.0, "forward_near")
    for q in range(4):
        add(31.0 + 4.6 * q, "forward_far", q)
        add(37.0 + 4.6 * q, "forward_last", q)
    add(18.0, "begin", tuple(range(n_near)))
    add(29.0, "begin", tuple(range(n_near, chunks)))
    add(43.0, "hidden", tuple(range(n_near)))
    add(53.0, "hidden", tuple(range(n_near, chunks - 1)))
    add(55.0, "hidden", (chunks - 1,))
    for k in range(chunks):
        far = k - n_near
        t = 18.0 + k * 0.4 if far < 0 else 29.0 + 0.5 * far
        t += 8.0 + 4.0 * (k if far < 0 else far)
        add(t, "middle", k)
        add(t + 6.0, "ready", k)
        add(t + 12.0, "spread", k)
        add(t + 17.0, "relay", k)
        add(max(t + 22.0, 60.0), "product", k)


def call_kernel(n_near, n_far, name, *args):
    smem = pl.BlockSpec(memory_space=pltpu.SMEM)
    hbm = pl.BlockSpec(memory_space=pl.ANY)
    n = n_near + n_far
    i16, f32, bf16 = jnp.int16, jnp.float32, jnp.bfloat16
    copies = 13 * n + 11 + 22 + 3 + 10
    return pl.pallas_call(
        functools.partial(kernel, n_near, n_far),
        out_shape=jax.ShapeDtypeStruct((3, 16), f32),
        in_specs=[smem] * 4 + [hbm] * 4,
        out_specs=pl.BlockSpec(memory_space=pltpu.VMEM),
        scratch_shapes=[
            pltpu.VMEM((ROWS, 1792), bf16),
            pltpu.VMEM((ROWS, 512), bf16),
            pltpu.VMEM((1024, 1792), bf16),
            pltpu.VMEM((1024, 512), bf16),
            pltpu.VMEM((n, ROWS, 128), f32),
            pltpu.VMEM((n, ROWS, 128), f32),
            pltpu.VMEM((n, 128, 1024), bf16),
            pltpu.VMEM((512, 128 * n_far), bf16),
            pltpu.VMEM((1792, 128 * n_far), bf16),
            pltpu.VMEM((n, 3, QUARTER + CODE, 128), i16),
            pltpu.VMEM((n, 3, QUARTER + CODE, 128), i16),
            pltpu.VMEM((n, 3, SLOT, 128), i16),
            pltpu.VMEM((n, 3, SLOT, 128), i16),
            pltpu.VMEM((n, 4, SLOT, 128), i16),
            pltpu.VMEM((n, 4 * BLOCK, 128), i16),
            pltpu.VMEM((2, 8, 128), f32),
            pltpu.VMEM((8, 8, 128), f32),
            pltpu.VMEM((8, 8, 128), f32),
            pltpu.VMEM((4, 8, 128), f32),
            pltpu.SemaphoreType.DMA((copies,)),
            pltpu.SemaphoreType.DMA((copies,)),
            pltpu.SemaphoreType.DMA((4,)),
        ],
        compiler_params=pltpu.CompilerParams(
            collective_id=n, has_side_effects=True, vmem_limit_bytes=56 * 2**20
        ),
        name=name,
    )(*args)


VARIANTS = ((4, 4), (2, 4), (2, 3))


def local(
    train_hidden,
    train_grad,
    val_hidden,
    val_grad,
    train_lengths,
    train_buckets,
    val_lengths,
    bucket_weight,
):
    args = (
        train_lengths,
        train_buckets,
        val_lengths,
        bucket_weight,
        train_hidden.reshape(HALF, 1792),
        train_grad.reshape(HALF, 512),
        val_hidden.reshape(128, 1792),
        val_grad.reshape(128, 512),
    )
    near = jnp.sum(val_lengths.reshape(2, 4, 2), axis=1)
    every = jnp.sum(near, axis=0, keepdims=True)
    fits = [
        jnp.all(every - jnp.minimum(near, 128 * a) <= 128 * b).astype(jnp.int32)
        for a, b in VARIANTS[1:]
    ]
    return lax.switch(
        sum(fits),
        [functools.partial(call_kernel, a, b, "ghost%d" % (a + b)) for a, b in VARIANTS],
        *args,
    )


def solution(mesh):
    placed = (
        P("dp", None, "tensor"),
        P("dp", None, "tensor"),
        P("dp", None, "tensor"),
        P("dp", None, "tensor"),
        P("dp"),
        P("dp"),
        P(),
        P(),
    )
    return jax.shard_map(
        local, mesh=mesh, in_specs=placed, out_specs=P("dp", None), check_vma=False
    )
```

time: 421 us -> 88.6 us (0.21)
  waiting for transfers between devices: 339 us -> 0 us
  Pallas kernels: 0 us -> 83.3 us
  blocking collectives: 41 us -> 0 us
  matrix products: 18.8 us -> 0 us
  between operations: 13.2 us -> 1.36 us
  other arithmetic: 5.29 us -> 0.75 us
    reduce_scatter x2 -> x0, waiting for transfers between devices: 186 us -> none  [the longest x1 98.6 us: local(): lax.psum_scatter(hidden_gram, 'tensor', scatter_dimension=0, tiled=True)]
    all_gather x2 -> x0, waiting for transfers between devices: 153 us -> none  [the longest x1 88.2 us: local(): lax.all_gather(val_masked, 'dp', axis=0, tiled=True)]
    pallas_call x0 -> x1, Pallas kernels: none -> 83.3 us  [call_kernel(): pl.pallas_call(functools.partial(kernel, n_near, n_far), out_shape=jax.Sh...]
    psum x1 -> x0, blocking collectives: 41 us -> none  [local(): pair_sum = lax.psum(partial_sum, 'tensor')]
    dot_general x4 -> x0, matrix products: 18.8 us -> none  [the longest x1 10.7 us: local(): lax.dot_general(train_flat, val_flat, contract, preferred_element_type=jn...]
  transfers between devices with their start and end apart: 4 -> 0, of which waited for: 4 -> 0; matrix products, arithmetic and copies ran while one was open for 5% -> 0% of each run, Pallas kernels for 0% -> 0%
where the time goes in v2:
time: 88.6 us; the launch traced here: 87.4 us
  Pallas kernels  83.3 us (94%)
  between operations  1.36 us (2%)
  local copies, waits for them, and re-layouts  1.32 us (1%)
    pallas_call x1, Pallas kernels, call_kernel(): pl.pallas_call(functools.partial(kernel, n_near, n_far), out_shape=jax.Sh...  83.3 us

profile of v2, /device:TPU:6, one launch (start us, length us, event | category | flops | bytes accessed | tf_op | source)
XLA Modules:
  0.0 87.4 jit_solution(5645723562978602334)
XLA Ops:
  0.0 0.7 reshape.16
  0.8 0.7 compare_reduce_fusion
  2.8 84.0 %conditional.1 = (f32[3,16]{1,0:T(4,128)S(1)}) conditional(s32[]{:T(128)} %clamp.3, (s32[3]{0:T(128)}, s32[3]{0:T(128)}, s32[16]{0:T(128)}, f32[4]{0:T(128)}, bf16[768,1792]{1,0:T(8,128)(2,1)}, /*index=5*/bf16[768,512]{1,0:T(8,128)(2,1)}, bf16[128,1792]{1,0:T(8,128)(2,1)}, bf16[128,512]{1,0:T(8,128)(2,1)}) %tuple.32, (s32[3]{0:T(128)}, ...), branch_computations={%region_4.0_spmd, %region_5.0_spmd, %region_6.0_spmd} | conditional | bytes 8 | solution.py:526
  3.3 83.3 %ghost5.1 = f32[3,16]{1,0:T(4,128)S(1)} custom-call(s32[3]{0:T(128)} %get-tuple-element.73.tl, s32[3]{0:T(128)} %get-tuple-element.74.tb, s32[16]{0:T(128)} %get-tuple-element.75.vl, f32[4]{0:T(128)} %get-tuple-element.76.bw, bf16[768,1792]{1,0:T(8,128)(2,1)} %get-tuple-element.77.th, bf16[768,512]{1,0:T(8,128)(2,1)} %get-tuple-element.78.tg, ...), custom_call_target="tpu_custom_call" | custom-call | tf_op jit(solution)/shard_map/cond/branch_2_fun/ghost5/pallas_call | solution.py:461
  86.8 0.6 copy.16
  (1 shorter events, 0.0 us)

commit v3 on v2

--- a/solution.py
+++ b/solution.py
@@ -23,6 +23,7 @@
 UP = 192
 TILE_G = 512
 TILE_H = 512
+IN_TURN = 48
 
 
 def quantize(x):
@@ -87,6 +88,12 @@
     sib = dev(c=1 - c)
     zhp = dev(zh=1 - zh)
     xp, xm, x2 = dev(x=(x + 1) % 4), dev(x=(x + 3) % 4), dev(x=(x + 2) % 4)
+    zhp2, xp2, xm2, x22 = (
+        (zhp, dev(zh=1 - zh, c=1 - c)),
+        (xp, dev(x=(x + 1) % 4, c=1 - c)),
+        (xm, dev(x=(x + 3) % 4, c=1 - c)),
+        (x2, dev(x=(x + 2) % 4, c=1 - c)),
+    )
     ys = [dev(y=(y + i) % 4) for i in (1, 2, 3)]
     zs = [dev(zl=(zl + i) % 4) for i in (1, 2, 3)]
     fin_y = [
@@ -99,10 +106,12 @@
     def send(src, dst, to):
         i = count[0]
         count[0] += 1
+        if i >= IN_TURN:
+            pending[i - IN_TURN].wait_send()
         copy = pltpu.make_async_remote_copy(
             src_ref=src,
             dst_ref=dst,
-            send_sem=ssem.at[i],
+            send_sem=ssem.at[i % IN_TURN],
             recv_sem=rsem.at[i],
             device_id=to,
             device_id_type=MESH,
@@ -112,9 +121,9 @@
         return copy
 
     own = [
-        pltpu.make_async_copy(vg, vg_b.at[pl.ds(0, 128)], lsem.at[0]),
+        pltpu.make_async_copy(vg.at[:, 0], vg_b.at[0, 0], lsem.at[0]),
         pltpu.make_async_copy(tg, tg_b.at[pl.ds(0, HALF)], lsem.at[1]),
-        pltpu.make_async_copy(vh, vh_b.at[pl.ds(0, 128)], lsem.at[2]),
+        pltpu.make_async_copy(vh.at[:, 0], vh_b.at[0, 0], lsem.at[2]),
         pltpu.make_async_copy(th, th_b.at[pl.ds(0, HALF)], lsem.at[3]),
     ]
     for copy in own:
@@ -124,23 +133,19 @@
     info[0] = jnp.where(row8 == 0, tl[0], jnp.where(row8 == 1, tl[1], tl[2])).astype(jnp.float32)
 
     barrier = pltpu.get_barrier_semaphore()
-    peers = [zhp, xp, xm, x2] + zs + fin_y
+    peers = [*zhp2, *xp2, *xm2, *x22] + zs + fin_y
     for peer in peers:
         pl.semaphore_signal(barrier, inc=1, device_id=peer, device_id_type=MESH)
     pl.semaphore_wait(barrier, len(peers))
 
-    def place(ref, s, part=0, parts=1):
-        return ref.at[pl.ds(128 * s + 128 // parts * part, 128 // parts)]
-
-    def piece(ref, part, parts):
-        return ref.at[pl.ds(128 // parts * part, 128 // parts)]
-
     arrived = {}
-    for h in range(2):
-        arrived["g", 4, h] = send(piece(vg, h, 2), place(vg_b, 4, h, 2), zhp)
-    arrived["g", 1] = send(vg, place(vg_b, 1), xp)
-    arrived["g", 2] = send(vg, place(vg_b, 2), xm)
-    arrived["g", 3] = send(vg, place(vg_b, 3), x2)
+    for e in range(2):
+        arrived["g", 4, e] = send(vg.at[:, e], vg_b.at[4, e], zhp2[e])
+    for e in range(2):
+        arrived["g", 1, e] = send(vg.at[:, e], vg_b.at[1, e], xp2[e])
+        arrived["g", 2, e] = send(vg.at[:, e], vg_b.at[2, e], xm2[e])
+        arrived["g", 3, e] = send(vg.at[:, e], vg_b.at[3, e], x22[e])
+    arrived["g", 0, 1] = send(vg.at[:, 1], vg_b.at[0, 1], sib)
     arrived["tg"] = send(tg, tg_b.at[pl.ds(HALF, HALF)], sib)
     arrived["info"] = send(info.at[0], info.at[1], sib)
 
@@ -149,11 +154,17 @@
     so_far = 0
     for s in range(8):
         r = (0, 1, 3, 2)[s % 4]
-        prompt = ((zh + s // 4) % 2) * 8 + ((x + 4 - r) % 4) * 2 + c
-        prompts.append(prompt)
-        lens.append(vl[prompt])
-        begins.append(so_far)
-        so_far = so_far + lens[s]
+        chip = ((zh + s // 4) % 2) * 8 + ((x + 4 - r) % 4) * 2
+        for e in range(2):
+            prompt = chip + (c + e) % 2
+            tokens = vl[prompt]
+            held = 0
+            for group in range(4):
+                held = held + jnp.clip(tokens - 32 * group - 16 * e, 0, 16)
+            prompts.append(prompt)
+            lens.append(held)
+            begins.append(so_far)
+            so_far = so_far + held
         if s == 3:
             near = so_far
     near_done = jnp.minimum(near, 128 * n_near)
@@ -169,14 +180,16 @@
         row = lax.broadcasted_iota(jnp.int32, (128, 128), 0)
         col = lax.broadcasted_iota(jnp.int32, (128, 128), 1)
         for s in range(places):
-            rank = col + begins[s]
-            hit = (rank - start == row) & (col < lens[s]) & (rank >= least)
+            first = col < 64
+            rank = col + jnp.where(first, begins[2 * s], begins[2 * s + 1] - 64)
+            end = jnp.where(first, lens[2 * s], lens[2 * s + 1] + 64)
+            hit = (rank - start == row) & (col < end) & (rank >= least)
             pick[k, :, pl.ds(128 * s, 128)] = jnp.where(hit, 1.0, 0.0).astype(jnp.bfloat16)
 
     def packed(k, ref, places):
         return lax.dot_general(
             pick[k, :, pl.ds(0, 128 * places)],
-            ref[pl.ds(0, 128 * places), :],
+            ref[pl.ds(0, places)].reshape(128 * places, ref.shape[-1]),
             (((1,), (0,)), ((), ())),
             preferred_element_type=jnp.float32,
         )
@@ -186,16 +199,21 @@
     def at(time, fn):
         ops.append((time, len(ops), fn))
 
+    def part(q):
+        return q // 2, pl.ds(q % 2 * 2, 2)
+
     def start_far():
         for q in range(4):
-            arrived["h", 4, q] = send(piece(vh, q, 4), place(vh_b, 4, q, 4), zhp)
+            e, groups = part(q)
+            arrived["h", 4, q] = send(vh.at[groups, e], vh_b.at[4, e, groups], zhp2[e])
 
     def start_near(h):
-        arrived["h", 1, h] = send(piece(vh, h, 2), place(vh_b, 1, h, 2), xp)
-        arrived["h", 2, 1 - h] = send(piece(vh, 1 - h, 2), place(vh_b, 2, 1 - h, 2), xm)
+        arrived["h", 1, h] = send(vh.at[:, h], vh_b.at[1, h], xp2[h])
+        arrived["h", 2, 1 - h] = send(vh.at[:, 1 - h], vh_b.at[2, 1 - h], xm2[1 - h])
 
     def start_train():
         arrived["th"] = send(th, th_b.at[pl.ds(HALF, HALF)], sib)
+        arrived["h", 0, 1] = send(vh.at[:, 1], vh_b.at[0, 1], sib)
 
     waited = set()
 
@@ -206,24 +224,26 @@
 
     def forward_near():
         have(("h", 1, 0))
-        arrived["h", 3, 0] = send(place(vh_b, 1, 0, 2), place(vh_b, 3, 0, 2), xp)
+        arrived["h", 3, 0] = send(vh_b.at[1, 0], vh_b.at[3, 0], xp)
         have(("h", 2, 1))
-        arrived["h", 3, 1] = send(place(vh_b, 2, 1, 2), place(vh_b, 3, 1, 2), xm)
+        arrived["h", 3, 1] = send(vh_b.at[2, 1], vh_b.at[3, 1], xm)
 
     def forward_far(q):
         have(("h", 4, q))
-        arrived["h", 5, q] = send(place(vh_b, 4, q, 4), place(vh_b, 5, q, 4), xp)
-        arrived["h", 6, q] = send(place(vh_b, 4, q, 4), place(vh_b, 6, q, 4), xm)
+        e, groups = part(q)
+        arrived["h", 5, q] = send(vh_b.at[4, e, groups], vh_b.at[5, e, groups], xp)
+        arrived["h", 6, q] = send(vh_b.at[4, e, groups], vh_b.at[6, e, groups], xm)
 
     def forward_last(q):
         s, to = (5, xp) if q % 2 == 0 else (6, xm)
         have(("h", s, q))
-        arrived["h", 7, q] = send(place(vh_b, s, q, 4), place(vh_b, 7, q, 4), to)
-
-    def forward_grad(h):
-        have(("g", 4, h))
+        e, groups = part(q)
+        arrived["h", 7, q] = send(vh_b.at[s, e, groups], vh_b.at[7, e, groups], to)
+
+    def forward_grad(e):
+        have(("g", 4, e))
         for s, to in ((5, xp), (6, xm), (7, x2)):
-            arrived["g", s, h] = send(place(vg_b, 4, h, 2), place(vg_b, s, h, 2), to)
+            arrived["g", s, e] = send(vg_b.at[4, e], vg_b.at[s, e], to)
 
     def mask_train():
         own[1].wait()
@@ -264,9 +284,10 @@
         places = chunk_range(ks[0])[2]
         if 0 in ks:
             own[0].wait()
+        have(("g", 0, 1))
         for s in range(1, places):
-            for key in (("g", s),) if s < 4 else (("g", s, 0), ("g", s, 1)):
-                have(key)
+            have(("g", s, 0))
+            have(("g", s, 1))
         for k in ks:
             fill_pick(k)
         multiply(ks, tg_b, vg_b, places, right_g, TILE_G, gram)
@@ -341,6 +362,7 @@
             own[2].wait()
             own[3].wait()
             have("th")
+        have(("h", 0, 1))
         for s in range(1, places):
             for i in range(2 if s < 4 else 4):
                 have(("h", s, i))
@@ -372,7 +394,7 @@
             tile = jnp.where(row8 == i, jnp.sum(sums[i], axis=0, keepdims=True), tile)
         start, least, places = chunk_range(k)
         rank = lane8 + start
-        for s in range(places):
+        for s in range(2 * places):
             mine = (rank >= begins[s]) & (rank < begins[s] + lens[s]) & (rank >= least)
             total[s] += jnp.where(mine, tile, 0.0)
 
@@ -398,7 +420,7 @@
         fn()
 
     mine = jnp.zeros((8, 128), jnp.float32)
-    for s in range(8):
+    for s in range(16):
         mine = jnp.where(lane8 == prompts[s], jnp.sum(total[s], axis=1, keepdims=True), mine)
     turned = jnp.where(row8 < 3, pltpu.roll(mine, 5, 0), pltpu.roll(mine, 3, 0))
     fin1[0] = jnp.where(c == 0, mine, turned)
@@ -417,7 +439,7 @@
         val_counts = jnp.where(lane8 == j, vl[j].astype(jnp.float32), val_counts)
     scores = pair * weight / (math.sqrt(FF * D) * jnp.sqrt(info[0] * val_counts))
     out[...] = scores[:3, :16]
-    for copy in pending:
+    for copy in pending[-IN_TURN:]:
         copy.wait_send()
 
 
@@ -425,31 +447,29 @@
     def add(time, name, *args):
         at(time, functools.partial(do[name], *args))
 
-    add(0.0, "start_far")
+    add(15.5, "start_far")
     add(0.1, "start_train")
-    add(0.2, "start_near", 0)
+    add(15.6, "start_near", 0)
     add(16.0, "mask_train")
     add(19.0, "forward_grad", 0)
     add(21.0, "forward_grad", 1)
     add(21.1, "start_near", 1)
-    add(29.0, "forward_near")
+    add(29.5, "forward_near")
     for q in range(4):
-        add(31.0 + 4.6 * q, "forward_far", q)
-        add(37.0 + 4.6 * q, "forward_last", q)
+        add([35.5, 39.0, 44.0, 48.0][q], "forward_far", q)
+        add([41.0, 45.0, 49.0, 53.0][q], "forward_last", q)
     add(18.0, "begin", tuple(range(n_near)))
-    add(29.0, "begin", tuple(range(n_near, chunks)))
-    add(43.0, "hidden", tuple(range(n_near)))
-    add(53.0, "hidden", tuple(range(n_near, chunks - 1)))
-    add(55.0, "hidden", (chunks - 1,))
+    add(27.0, "begin", tuple(range(n_near, chunks)))
+    add(47.0, "hidden", tuple(range(n_near)))
+    add(55.0, "hidden", tuple(range(n_near, chunks - 1)))
+    add(58.5, "hidden", (chunks - 1,))
     for k in range(chunks):
         far = k - n_near
-        t = 18.0 + k * 0.4 if far < 0 else 29.0 + 0.5 * far
-        t += 8.0 + 4.0 * (k if far < 0 else far)
-        add(t, "middle", k)
-        add(t + 6.0, "ready", k)
-        add(t + 12.0, "spread", k)
-        add(t + 17.0, "relay", k)
-        add(max(t + 22.0, 60.0), "product", k)
+        near_times = [t + 0.5 * k for t in [30, 37, 43, 48, 65]]
+        far_times = [t + 4.0 * far for t in [38.2, 44.5, 50, 55, 66.0]]
+        names = ("middle", "ready", "spread", "relay", "product")
+        for t, name in zip(near_times if far < 0 else far_times, names):
+            add(t, name, k)
 
 
 def call_kernel(n_near, n_far, name, *args):
@@ -457,7 +477,7 @@
     hbm = pl.BlockSpec(memory_space=pl.ANY)
     n = n_near + n_far
     i16, f32, bf16 = jnp.int16, jnp.float32, jnp.bfloat16
-    copies = 13 * n + 11 + 22 + 3 + 10
+    copies = 13 * n + 51
     return pl.pallas_call(
         functools.partial(kernel, n_near, n_far),
         out_shape=jax.ShapeDtypeStruct((3, 16), f32),
@@ -466,8 +486,8 @@
         scratch_shapes=[
             pltpu.VMEM((ROWS, 1792), bf16),
             pltpu.VMEM((ROWS, 512), bf16),
-            pltpu.VMEM((1024, 1792), bf16),
-            pltpu.VMEM((1024, 512), bf16),
+            pltpu.VMEM((8, 2, 4, 16, 1792), bf16),
+            pltpu.VMEM((8, 2, 4, 16, 512), bf16),
             pltpu.VMEM((n, ROWS, 128), f32),
             pltpu.VMEM((n, ROWS, 128), f32),
             pltpu.VMEM((n, 128, 1024), bf16),
@@ -480,10 +500,10 @@
             pltpu.VMEM((n, 4, SLOT, 128), i16),
             pltpu.VMEM((n, 4 * BLOCK, 128), i16),
             pltpu.VMEM((2, 8, 128), f32),
-            pltpu.VMEM((8, 8, 128), f32),
+            pltpu.VMEM((16, 8, 128), f32),
             pltpu.VMEM((8, 8, 128), f32),
             pltpu.VMEM((4, 8, 128), f32),
-            pltpu.SemaphoreType.DMA((copies,)),
+            pltpu.SemaphoreType.DMA((IN_TURN,)),
             pltpu.SemaphoreType.DMA((copies,)),
             pltpu.SemaphoreType.DMA((4,)),
         ],
@@ -494,7 +514,7 @@
     )(*args)
 
 
-VARIANTS = ((4, 4), (2, 4), (2, 3))
+VARIANTS = ((4, 4), (2, 3), (2, 2))
 
 
 def local(
@@ -514,11 +534,15 @@
         bucket_weight,
         train_hidden.reshape(HALF, 1792),
         train_grad.reshape(HALF, 512),
-        val_hidden.reshape(128, 1792),
-        val_grad.reshape(128, 512),
+        val_hidden.reshape(4, 2, 16, 1792),
+        val_grad.reshape(4, 2, 16, 512),
     )
-    near = jnp.sum(val_lengths.reshape(2, 4, 2), axis=1)
-    every = jnp.sum(near, axis=0, keepdims=True)
+    prompt = jnp.arange(16)[None, :]
+    row = jnp.arange(4)[:, None]
+    stay = sum(jnp.clip(val_lengths - 32 * group, 0, 16) for group in range(4))[None, :]
+    held = jnp.where(prompt % 2 == row % 2, stay, val_lengths[None, :] - stay)
+    near = jnp.sum(jnp.where(prompt // 8 == row // 2, held, 0), axis=1)
+    every = jnp.sum(held, axis=1)
     fits = [
         jnp.all(every - jnp.minimum(near, 128 * a) <= 128 * b).astype(jnp.int32)
         for a, b in VARIANTS[1:]

time: 88.6 us -> 83.8 us (0.946)
  Pallas kernels: 83.3 us -> 78 us
    pallas_call x1, Pallas kernels: 83.3 us -> 78 us  [call_kernel(): pl.pallas_call(functools.partial(kernel, n_near, n_far), out_shape=jax.Sh...]
where the time goes in v3:
time: 83.8 us; the launch traced here: 82.3 us
  Pallas kernels  78 us (93%)
  other arithmetic  1.62 us (2%)
  between operations  1.36 us (2%)
    pallas_call x1, Pallas kernels, call_kernel(): pl.pallas_call(functools.partial(kernel, n_near, n_far), out_shape=jax.Sh...  78 us

profile of v3, /device:TPU:6, one launch (start us, length us, event | category | flops | bytes accessed | tf_op | source)
XLA Modules:
  0.0 82.3 jit_solution(17207175214737097472)
XLA Ops:
  0.0 0.7 fusion.1
  0.7 0.2 fusion
  0.9 0.7 compare_reduce_fusion
  3.0 78.7 %conditional.1 = (f32[3,16]{1,0:T(4,128)S(1)}) conditional(s32[]{:T(128)} %clamp.7, (s32[3]{0:T(128)}, s32[3]{0:T(128)}, s32[16]{0:T(128)}, f32[4]{0:T(128)}, bf16[768,1792]{1,0:T(8,128)(2,1)}, /*index=5*/bf16[768,512]{1,0:T(8,128)(2,1)}, bf16[4,2,16,1792]{3,2,1,0:T(8,128)(2,1)}, bf16[4,2,16,512]{3,2,1,0:T(8,128)(2,1)}) %tuple.35, ...), branch_computations={%region_4.5_spmd, %region_5.6_spmd, %region_6.7_spmd} | conditional | bytes 8 | solution.py:550
  3.4 78.0 %ghost4.1 = f32[3,16]{1,0:T(4,128)S(1)} custom-call(s32[3]{0:T(128)} %get-tuple-element.73.tl, s32[3]{0:T(128)} %get-tuple-element.74.tb, s32[16]{0:T(128)} %get-tuple-element.75.vl, f32[4]{0:T(128)} %get-tuple-element.76.bw, bf16[768,1792]{1,0:T(8,128)(2,1)} %get-tuple-element.77.th, bf16[768,512]{1,0:T(8,128)(2,1)} %get-tuple-element.78.tg, ...), custom_call_target="tpu_custom_call" | custom-call | tf_op jit(solution)/shard_map/cond/branch_2_fun/ghost4/pallas_call | solution.py:481
  81.7 0.6 copy.16
  (2 shorter events, 0.0 us)

commit v4 on v3

--- a/solution.py
+++ b/solution.py
@@ -514,7 +514,7 @@
     )(*args)
 
 
-VARIANTS = ((4, 4), (2, 3), (2, 2))
+VARIANTS = ((4, 4), (2, 4), (2, 3))
 
 
 def local(

time: 83.8 us -> 87.7 us (1.047)
  Pallas kernels: 78 us -> 82.4 us
    pallas_call x1, Pallas kernels: 78 us -> 82.4 us  [call_kernel(): pl.pallas_call(functools.partial(kernel, n_near, n_far), out_shape=jax.Sh...]
where the time goes in v4:
time: 87.7 us; the launch traced here: 86.7 us
  Pallas kernels  82.4 us (94%)
  other arithmetic  1.62 us (2%)
  between operations  1.36 us (2%)
    pallas_call x1, Pallas kernels, call_kernel(): pl.pallas_call(functools.partial(kernel, n_near, n_far), out_shape=jax.Sh...  82.4 us

profile of v4, /device:TPU:6, one launch (start us, length us, event | category | flops | bytes accessed | tf_op | source)
XLA Modules:
  0.0 86.7 jit_solution(1570971538260006864)
XLA Ops:
  0.0 0.7 fusion.1
  0.7 0.2 fusion
  0.9 0.7 compare_reduce_fusion
  3.0 83.1 %conditional.1 = (f32[3,16]{1,0:T(4,128)S(1)}) conditional(s32[]{:T(128)} %clamp.7, (s32[3]{0:T(128)}, s32[3]{0:T(128)}, s32[16]{0:T(128)}, f32[4]{0:T(128)}, bf16[768,1792]{1,0:T(8,128)(2,1)}, /*index=5*/bf16[768,512]{1,0:T(8,128)(2,1)}, bf16[4,2,16,1792]{3,2,1,0:T(8,128)(2,1)}, bf16[4,2,16,512]{3,2,1,0:T(8,128)(2,1)}) %tuple.35, ...), branch_computations={%region_4.5_spmd, %region_5.6_spmd, %region_6.7_spmd} | conditional | bytes 8 | solution.py:550
  3.4 82.4 %ghost5.1 = f32[3,16]{1,0:T(4,128)S(1)} custom-call(s32[3]{0:T(128)} %get-tuple-element.73.tl, s32[3]{0:T(128)} %get-tuple-element.74.tb, s32[16]{0:T(128)} %get-tuple-element.75.vl, f32[4]{0:T(128)} %get-tuple-element.76.bw, bf16[768,1792]{1,0:T(8,128)(2,1)} %get-tuple-element.77.th, bf16[768,512]{1,0:T(8,128)(2,1)} %get-tuple-element.78.tg, ...), custom_call_target="tpu_custom_call" | custom-call | tf_op jit(solution)/shard_map/cond/branch_2_fun/ghost5/pallas_call | solution.py:481
  86.1 0.6 copy.16
  (2 shorter events, 0.0 us)
